TPU v7x, 256 devices: a whole 4x4x8 slice. The times are simulated.
256 devices in a mesh: blk: 128 (over z, y_hi, x, core), feat: 2 (over y_lo).
Axes of the slice: x: 4, y: 4 (y_hi: 2, y_lo: 2; y = y_hi * 2 + y_lo), z: 8, core: 2. Of those that a mesh axis runs over, the one named last changes fastest.
Arguments:
- images: bfloat16 [131072, 1152], P('blk', 'feat'), may hold values from -1 to 1
- texts: bfloat16 [2048, 1152], P('blk', 'feat'), may hold values from -1 to 1
- img_group: int32 [1024], replicated, may hold values from 0 to 31
- txt_group: int32 [16], replicated, may hold values from 0 to 31
- temp: float32 [], replicated, may hold values from 2 to 4
- bias: float32 [], replicated, may hold values from -3 to -1
- loss_scale: float32 [], replicated, may hold values from 16384 to 65536
Outputs:
- grad_images: float32 [131072, 1152], P('blk', 'feat')
- grad_texts: float32 [2048, 1152], P('blk', 'feat')
All inputs are finite; a program needn't handle non-finite values.
Results may differ from a plain program's by a relative error of at most 0.0023.
Values may be sent and summed in bfloat16 or wider, within the bound.
A program may use at most 64 MiB of HBM per device.

v0:
```python
import jax
import jax.numpy as jnp
from jax import lax
from jax.sharding import PartitionSpec as P


def row_groups(first_rows, txt_group):
    blocks = first_rows // 128
    table = jnp.arange(txt_group.shape[0], dtype=jnp.int32)
    onehot = (blocks[:, None] == table[None, :]).astype(jnp.int32)
    return jnp.sum(onehot * txt_group[None, :], axis=1)


def loss_weights(logits, groups_rows, groups_cols, factor):
    sign = jnp.where(groups_rows[:, None] == groups_cols[None, :], 1.0, -1.0).astype(jnp.float32)
    return (factor * sign * jax.nn.sigmoid(-sign * logits)).astype(jnp.bfloat16)


def body(images, texts, img_group, txt_group, temp, bias, loss_scale):
    nblk = lax.axis_size("blk")
    me = lax.axis_index("blk")
    fidx = lax.axis_index("feat")
    cols = images.shape[0]
    txt_rows = texts.shape[0]
    total_texts = txt_rows * nblk
    total_images = cols * nblk
    local_groups = lax.dynamic_slice_in_dim(img_group, me * (cols // 128), cols // 128)
    col_group = jnp.repeat(local_groups, 128, total_repeat_length=cols)
    factor = -(loss_scale * temp / total_images)
    all_texts = lax.all_gather(texts, "blk", axis=0, tiled=True)
    partial_value = lax.dot_general(
        all_texts, images, (((1,), (1,)), ((), ())), preferred_element_type=jnp.float32
    )
    share = lax.psum_scatter(partial_value, "feat", scatter_dimension=1, tiled=True)
    width_share = share.shape[1]
    own_cols = lax.dynamic_slice_in_dim(col_group, fidx * width_share, width_share)
    groups_rows = row_groups(jnp.arange(total_texts, dtype=jnp.int32), txt_group)
    part_weights = loss_weights(temp * share + bias, groups_rows, own_cols, factor)
    weight_store = lax.all_gather(part_weights, "feat", axis=1, tiled=True)
    grad_images = lax.dot_general(
        weight_store, all_texts, (((0,), (0,)), ((), ())), preferred_element_type=jnp.float32
    )
    block = lax.slice_in_dim(weight_store, 0, txt_rows * lax.axis_size("blk"), axis=0)
    grad_texts = lax.psum_scatter(
        jnp.dot(block, images, preferred_element_type=jnp.float32),
        "blk",
        scatter_dimension=0,
        tiled=True,
    )
    return (grad_images, grad_texts)


def solution(mesh):
    in_specs = (P("blk", "feat"), P("blk", "feat"), P(), P(), P(), P(), P())
    out_specs = (P("blk", "feat"), P("blk", "feat"))
    return jax.shard_map(body, mesh=mesh, in_specs=in_specs, out_specs=out_specs, check_vma=False)
```

profile of v0, /device:TPU:8, one launch (start us, length us, event | category | flops | bytes accessed | tf_op | source)
XLA Modules:
  0.0 987.8 jit_solution(2951376125258196295)
XLA Ops:
  7.2 0.0 copy-start
  7.2 0.0 all-gather.3.cloned.1.call-start
  7.2 0.7 all-gather.3.cloned.1.call-update
  7.9 0.0 reduce-scatter.3.cloned.1.call-start
  8.0 121.9 %all-gather.3.cloned.1.call-done = bf16[2048,576]{1,0:T(8,128)(2,1)} async-done(((bf16[16,576]{1,0:T(8,128)(2,1)}), bf16[2048,576]{1,0:T(8,128)(2,1)}) %all-gather.3.cloned.1.call-update) | async-done | bytes 2359312 | tf_op jit(solution)/shard_map/all_gather | solution.py:30
  129.9 0.0 copy-done
  129.9 7.4 fusion.13
  137.3 0.0 reduce-scatter.3.cloned.1.call-update
  137.4 0.0 all-gather.5.cloned.1.call-start
  139.4 0.8 dynamic_slice.6
  140.1 0.7 fusion.12
  140.8 4.5 compare_select_fusion.1
  145.3 0.7 select_select_fusion
  146.0 0.1 dynamic_slice.7
  146.1 0.1 select_reduce_fusion
  146.2 91.7 %reduce-scatter.3.cloned.1.call-done = f32[2048,512]{1,0:T(8,128)} async-done(((f32[2048,1024]{1,0:T(8,128)}), f32[2048,512]{1,0:T(8,128)}) %reduce-scatter.3.cloned.1.call-update) | async-done | bytes 4194320 | tf_op jit(solution)/shard_map/reduce_scatter | solution.py:34
  237.8 4.4 fusion.1
  242.2 0.0 all-gather.5.cloned.1.call-update
  242.2 0.0 reduce-scatter.5.cloned.1.call-start
  242.3 62.9 %all-gather.5.cloned.1.call-done = bf16[2048,1024]{1,0:T(8,128)(2,1)} async-done(((bf16[2048,512]{1,0:T(8,128)(2,1)}), bf16[2048,1024]{1,0:T(8,128)(2,1)}) %all-gather.5.cloned.1.call-update) | async-done | bytes 4194320 | tf_op jit(solution)/shard_map/all_gather | solution.py:39
  305.2 8.0 fusion.15
  313.2 0.0 reduce-scatter.5.cloned.1.call-update
  313.2 7.1 fusion.14
  320.3 661.0 %reduce-scatter.5.cloned.1.call-done = f32[16,576]{1,0:T(8,128)} async-done(((f32[2048,576]{1,0:T(8,128)}), f32[16,576]{1,0:T(8,128)}) %reduce-scatter.5.cloned.1.call-update) | async-done | bytes 36880 | tf_op jit(solution)/shard_map/reduce_scatter | solution.py:44
  (6 shorter events, 0.0 us)
Async XLA Ops:
  7.2 122.7 %copy-start = (bf16[1024,576]{0,1:T(8,128)(2,1)S(1)}, bf16[1024,576]{0,1:T(8,128)(2,1)}, u32[]{:S(2)}) copy-start(bf16[1024,576]{0,1:T(8,128)(2,1)} %param.9) | copy-start | bytes 3538948
  7.2 122.7 %all-gather.3.cloned.1.call-start = ((), (), s32[]{:S(2)}) async-start(), calls=%async_computation.2 | async-start | bytes 2641920 | tf_op jit(solution)/shard_map/all_gather | solution.py:30
  7.9 229.9 %reduce-scatter.3.cloned.1.call-start = ((), (), s32[]{:S(2)}) async-start(), calls=%async_computation.3 | async-start | bytes 12582912 | tf_op jit(solution)/shard_map/reduce_scatter | solution.py:34
  137.3 8.7 copy-start.1
  137.4 167.9 %all-gather.5.cloned.1.call-start = ((), (), s32[]{:S(2)}) async-start(), calls=%async_computation.4 | async-start | bytes 6291456 | tf_op jit(solution)/shard_map/all_gather | solution.py:39
  242.2 739.0 %reduce-scatter.5.cloned.1.call-start = ((), (), s32[]{:S(2)}) async-start(), calls=%async_computation.5 | async-start | bytes 5283840 | tf_op jit(solution)/shard_map/reduce_scatter | solution.py:44
Sparse Core Ops, SparseCore 0:
  11.9 117.9 all-gather.2
  137.5 100.2 reduce-scatter.2
  242.4 62.8 all-gather.4
  313.3 667.8 reduce-scatter.4
where the time goes:
time: 988 us
  waiting for transfers between devices  938 us (95%)
  matrix products  22.5 us (2%)
  between operations  15.7 us (2%)
    reduce_scatter x1, waiting for transfers between devices, body(): lax.psum_scatter(jnp.dot(block, images, preferred_element_type=jnp.float3...  661 us
    all_gather x1, waiting for transfers between devices, body(): all_texts = lax.all_gather(texts, 'blk', axis=0, tiled=True)  122 us
    reduce_scatter x1, waiting for transfers between devices, body(): lax.psum_scatter(partial_value, 'feat', scatter_dimension=1, tiled=True)  91.7 us
    all_gather x1, waiting for transfers between devices, body(): weight_store = lax.all_gather(part_weights, 'feat', axis=1, tiled=True)  62.9 us
  transfers between devices with their start and end apart: 4, of which 4 were waited for; matrix products, arithmetic and copies ran while one was open for 1% of the time, Pallas kernels for 0%

commit v1 on v0

v1 whole, which is shorter than its diff:
```python
import functools

import jax
import jax.numpy as jnp
from jax import lax
from jax.experimental import pallas as pl
from jax.experimental.pallas import tpu as pltpu
from jax.sharding import PartitionSpec as P

MESH = pl.DeviceIdType.MESH
NZ, NY, NX = 8, 2, 4
R = 16
CH = 256


def chain_lengths(n):
    return n // 2, (n - 1) // 2


def kernel(
    cfg,
    img_ref, txt_ref, ig_ref, tg_ref, temp_ref, bias_ref, scale_ref,
    gi_out, gt_out,
    T, TT, I, W, G, gI, gIr, tgv, tp,
    rAzf, rAzb, rAxf, rAxb, rBxf, rBxb, rBzf, rBzb, rY, finY,
    send, recv, loc,
):
    nz, ny, nx, F, FP, C, total_images = cfg
    HALF = nz * nx * R
    ROWS = 2 * HALF
    NCH = C // CH
    blk = lax.axis_index("blk")
    feat = lax.axis_index("feat")
    core = lax.rem(blk, 2)
    x = lax.rem(blk // 2, nx)
    yh = lax.rem(blk // (2 * nx), ny)
    z = blk // (2 * nx * ny)
    step_dir = 1 - 2 * core

    def at(z_, yh_, x_, core_, feat_):
        return (((z_ * ny + yh_) * nx + x_) * 2 + core_, feat_)

    def zz(k):
        return lax.rem(z + step_dir * k + 2 * nz, nz)

    def xx(k):
        return lax.rem(x + step_dir * k + 2 * nx, nx)

    sibling = at(z, yh, x, 1 - core, feat)
    dev_f = at(z, yh, x, core, 1 - feat)
    dev_y = at(z, 1 - yh, x, core, feat)
    dev_d = at(z, 1 - yh, x, core, 1 - feat)
    zf, zb = at(zz(1), yh, x, core, feat), at(zz(-1), yh, x, core, feat)
    xf, xb = at(z, yh, xx(1), core, feat), at(z, yh, xx(-1), core, feat)

    barrier = pltpu.get_barrier_semaphore()
    partners = (sibling, dev_f, dev_y, dev_d, zf, zb, xf, xb)
    for dev in partners:
        pl.semaphore_signal(barrier, inc=1, device_id=dev, device_id_type=MESH)
    pl.semaphore_wait(barrier, len(partners))

    count = [0]
    started = []

    def copy_to(src, dst, dev):
        i = count[0]
        count[0] += 1
        c = pltpu.make_async_remote_copy(
            src_ref=src, dst_ref=dst, send_sem=send.at[i], recv_sem=recv.at[i], device_id=dev, device_id_type=MESH
        )
        c.start()
        started.append(c)
        return c

    tp[...] = jnp.zeros_like(tp)
    tp[:, 0:F] = txt_ref[...]

    def rowsA(z_, x_):
        return pl.multiple_of((z_ * nx + x_) * R, R)

    def rowsB(z_, x_):
        return pl.multiple_of(HALF + (x_ * nz + z_) * R, R)

    myrow = pl.multiple_of(jnp.where(yh == 0, rowsA(z, x), rowsB(z, x)), R)
    mylane = pl.multiple_of(feat * FP, 128)
    T[pl.ds(myrow, R), pl.ds(mylane, FP)] = tp[...]
    own_dst = T.at[pl.ds(myrow, R), pl.ds(mylane, FP)]
    y_copies = [copy_to(tp, own_dst, dev) for dev in (dev_f, dev_y, dev_d)]

    frow = pl.multiple_of(feat * FP, 16)
    orow = pl.multiple_of((1 - feat) * FP, 16)
    img_copies = []
    for j in range(NCH):
        cols = pl.ds(j * CH, CH)
        img_copies.append(copy_to(img_ref.at[:, cols], I.at[core, pl.ds(frow, F), cols], dev_f))
    sib_own = copy_to(img_ref, I.at[core, pl.ds(frow, F), :], sibling)
    own_copy = pltpu.make_async_copy(img_ref, I.at[core, pl.ds(frow, F), :], loc.at[0])
    own_copy.start()

    for r in range(2):
        for f in range(2):
            I[r, f * FP + F : (f + 1) * FP, :] = jnp.zeros((FP - F, C), jnp.bfloat16)

    def fill_groups(i, carry):
        za, xb_ = i // nx, i // nz
        tgv[pl.ds(pl.multiple_of(i * R, R), R), :] = jnp.full((R, 128), tg_ref[za * ny], jnp.int32)
        zb_ = i - xb_ * nz
        tgv[pl.ds(pl.multiple_of(HALF + i * R, R), R), :] = jnp.full((R, 128), tg_ref[zb_ * ny + 1], jnp.int32)
        return carry

    lax.fori_loop(0, nz * nx, fill_groups, 0)

    def blockAx(k):
        return T.at[pl.ds(rowsA(z, xx(k)), R), :]

    def blockAz(k):
        return T.at[pl.ds(rowsA(zz(k), 0), nx * R), :]

    def blockBz(k):
        return T.at[pl.ds(rowsB(zz(k), x), R), :]

    def blockBx(k):
        return T.at[pl.ds(rowsB(0, xx(k)), nz * R), :]

    class Gather:
        def __init__(self, block, fwd, bwd, n):
            self.block, self.fwd, self.bwd = block, fwd, bwd
            self.lf, self.lb = chain_lengths(n)
            self.cf, self.cb = [], []

        def send(self, s):
            if s < self.lf:
                self.cf.append(copy_to(self.block(-s), self.block(-s), self.fwd))
            if s < self.lb:
                self.cb.append(copy_to(self.block(s), self.block(s), self.bwd))

        def wait(self, s):
            if s < self.lf:
                self.cf[s].wait_recv()
            if s < self.lb:
                self.cb[s].wait_recv()

    gAx, gAz = Gather(blockAx, xf, xb, nx), Gather(blockAz, zf, zb, nz)
    gBx, gBz = Gather(blockBx, xf, xb, nx), Gather(blockBz, zf, zb, nz)
    lx, lz = nx // 2, nz // 2

    for c in y_copies:
        c.wait_recv()
    gAx.send(0)
    gBz.send(0)
    for s in range(lx):
        gAx.wait(s)
        gAx.send(s + 1)
        gBz.wait(s)
        gBz.send(s + 1)
    gAz.send(0)
    for s in range(lx, lz):
        gBz.wait(s)
        gBz.send(s + 1)
    gBx.send(0)
    for s in range(lz):
        gAz.wait(s)
        gAz.send(s + 1)
        if s < lx:
            gBx.wait(s)
            gBx.send(s + 1)

    def transpose_rows(i, carry):
        rows = pl.ds(pl.multiple_of(i * 128, 128), 128)
        TT[:, rows] = T[rows, pl.ds(mylane, FP)].T
        return carry

    lax.fori_loop(0, ROWS // 128, transpose_rows, 0)

    own_copy.wait()
    sib_own.wait_recv()

    temp, bias = temp_ref[0], bias_ref[0]
    factor = -(scale_ref[0] * temp / total_images)
    base = count[0]
    count[0] += 2 * NCH
    TM = min(256, ROWS)
    FM = F // 3

    def fwd_copy(j):
        cols = pl.ds(pl.multiple_of(j * CH, CH), CH)
        ref = I.at[core, pl.ds(orow, F), cols]
        return pltpu.make_async_remote_copy(
            src_ref=ref, dst_ref=ref, send_sem=send.at[base + j], recv_sem=recv.at[base + j], device_id=sibling, device_id_type=MESH
        )

    def gi_copy(j):
        cols = pl.ds(pl.multiple_of(j * CH, CH), CH)
        return pltpu.make_async_remote_copy(
            src_ref=gI.at[1, :, cols], dst_ref=gIr.at[:, cols],
            send_sem=send.at[base + NCH + j], recv_sem=recv.at[base + NCH + j], device_id=sibling, device_id_type=MESH,
        )

    def img_wait(j):
        cols = pl.ds(pl.multiple_of(j * CH, CH), CH)
        return pltpu.make_async_remote_copy(
            src_ref=img_ref.at[:, cols], dst_ref=I.at[core, pl.ds(frow, F), cols],
            send_sem=send.at[3 + j], recv_sem=recv.at[3 + j], device_id=dev_f, device_id_type=MESH,
        )

    def step(k, carry):
        j = k // 2
        which = lax.rem(k, 2)
        r = jnp.where(which == 0, core, 1 - core)
        cols = pl.ds(pl.multiple_of(j * CH, CH), CH)

        @pl.when(which == 0)
        def _():
            img_wait(j).wait_recv()
            fwd_copy(j).start()

        @pl.when(which == 1)
        def _():
            fwd_copy(j).wait_recv()

        first_group = (blk - core + r) * (C // 128) + j * (CH // 128)

        def tile(m, carry2):
            rows = pl.ds(pl.multiple_of(m * TM, TM), TM)
            raw = jnp.dot(T[rows, :], I[r, :, cols], preferred_element_type=jnp.float32)
            tg = tgv[rows, :]
            for q in range(CH // 128):
                logit = temp * raw[:, q * 128 : (q + 1) * 128] + bias
                same = tg == ig_ref[first_group + q]
                p = 1.0 / (1.0 + jnp.exp(jnp.where(same, logit, -logit)))
                W[rows, q * 128 : (q + 1) * 128] = (jnp.where(same, factor, -factor) * p).astype(jnp.bfloat16)
            part = lax.dot_general(
                W[rows, :], I[r, pl.ds(frow, FP), cols], (((1,), (1,)), ((), ())), preferred_element_type=jnp.float32
            )

            @pl.when(k == 0)
            def _():
                G[rows, :] = part

            @pl.when(k != 0)
            def _():
                G[rows, :] = G[rows, :] + part

            return carry2

        lax.fori_loop(0, ROWS // TM, tile, 0)

        def gi_tile(m, carry2):
            rows = pl.ds(pl.multiple_of(m * FM, 16), FM)
            gI[which, rows, cols] = jnp.dot(TT[rows, :], W[...], preferred_element_type=jnp.float32)
            return carry2

        lax.fori_loop(0, 3, gi_tile, 0)

        @pl.when(which == 1)
        def _():
            gi_copy(j).start()

        return carry

    lax.fori_loop(0, 2 * NCH, step, 0)

    class Reduce:
        def __init__(self, block, rf, rb, fwd, bwd, n):
            self.block, self.rf, self.rb, self.fwd, self.bwd = block, rf, rb, fwd, bwd
            self.lf, self.lb = chain_lengths(n)
            self.cf, self.cb = [], []

        def send(self, s):
            if s < self.lf:
                src = self.block(self.lf - s)
                if s > 0:
                    self.rf[s - 1, :, :] = self.rf[s - 1] + src[...]
                    src = self.rf.at[s - 1]
                self.cf.append(copy_to(src, self.rf.at[s], self.fwd))
            if s < self.lb:
                src = self.block(-(self.lb - s))
                if s > 0:
                    self.rb[s - 1, :, :] = self.rb[s - 1] + src[...]
                    src = self.rb.at[s - 1]
                self.cb.append(copy_to(src, self.rb.at[s], self.bwd))

        def wait(self, s):
            if s < self.lf:
                self.cf[s].wait_recv()
            if s < self.lb:
                self.cb[s].wait_recv()

        def finish(self):
            total = self.rf[self.lf - 1] + self.block(0)[...]
            if self.lb:
                total = total + self.rb[self.lb - 1]
            self.rf[self.lf - 1, :, :] = total
            return self.rf.at[self.lf - 1]

    def rAz(k):
        return G.at[pl.ds(rowsA(zz(k), 0), nx * R), :]

    def rBx(k):
        return G.at[pl.ds(rowsB(0, xx(k)), nz * R), :]

    sAz = Reduce(rAz, rAzf, rAzb, zf, zb, nz)
    sBx = Reduce(rBx, rBxf, rBxb, xf, xb, nx)
    sAz.send(0)
    sBx.send(0)
    for s in range(lx):
        sAz.wait(s)
        sAz.send(s + 1)
        sBx.wait(s)
        sBx.send(s + 1)
    totB = sBx.finish()
    sBz = Reduce(lambda k: totB.at[pl.ds(pl.multiple_of(zz(k) * R, R), R), :], rBzf, rBzb, zf, zb, nz)
    sBz.send(0)

    out_copies = []
    for j in range(NCH):
        cols = pl.ds(j * CH, CH)
        gi_copy(j).wait_recv()
        gI[0, :, cols] = gI[0, :, cols] + gIr[:, cols]
        c = pltpu.make_async_copy(gI.at[0, :, cols], gi_out.at[:, cols], loc.at[1 + j])
        c.start()
        out_copies.append(c)

    for s in range(lx, lz):
        sAz.wait(s)
        sAz.send(s + 1)
        sBz.wait(s - lx)
        sBz.send(s - lx + 1)
    totA = sAz.finish()
    sAx = Reduce(lambda k: totA.at[pl.ds(pl.multiple_of(xx(k) * R, R), R), :], rAxf, rAxb, xf, xb, nx)
    sAx.send(0)
    for s in range(lx):
        sAx.wait(s)
        sAx.send(s + 1)
        sBz.wait(lz - lx + s)
        sBz.send(lz - lx + s + 1)
    endA, endB = sAx.finish(), sBz.finish()
    mineA = (yh == 0).astype(jnp.float32)
    a, b = endA[...], endB[...]
    finY[...] = b * mineA + a * (1.0 - mineA)
    last = copy_to(finY, rY, dev_y)
    own = a * mineA + b * (1.0 - mineA)
    last.wait_recv()
    gt_out[...] = (own + rY[...])[:, 0:F]

    for c in started:
        c.wait_send()
    for j in range(NCH):
        fwd_copy(j).wait_send()
        gi_copy(j).wait_send()
    for c in out_copies:
        c.wait()


def build(nz, ny, nx, F, FP, C, total_images):
    lfx, lbx = chain_lengths(nx)
    lfz, lbz = chain_lengths(nz)
    rows = 2 * nz * nx * R
    f32, bf16 = jnp.float32, jnp.bfloat16
    scratch = [
        pltpu.VMEM((rows, 2 * FP), bf16),
        pltpu.VMEM((FP, rows), bf16),
        pltpu.VMEM((2, 2 * FP, C), bf16),
        pltpu.VMEM((rows, CH), bf16),
        pltpu.VMEM((rows, FP), f32),
        pltpu.VMEM((2, F, C), f32),
        pltpu.VMEM((F, C), f32),
        pltpu.VMEM((rows, 128), jnp.int32),
        pltpu.VMEM((R, FP), bf16),
        pltpu.VMEM((lfz, nx * R, FP), f32),
        pltpu.VMEM((max(lbz, 1), nx * R, FP), f32),
        pltpu.VMEM((lfx, R, FP), f32),
        pltpu.VMEM((max(lbx, 1), R, FP), f32),
        pltpu.VMEM((lfx, nz * R, FP), f32),
        pltpu.VMEM((max(lbx, 1), nz * R, FP), f32),
        pltpu.VMEM((lfz, R, FP), f32),
        pltpu.VMEM((max(lbz, 1), R, FP), f32),
        pltpu.VMEM((R, FP), f32),
        pltpu.VMEM((R, FP), f32),
        pltpu.SemaphoreType.DMA((80,)),
        pltpu.SemaphoreType.DMA((80,)),
        pltpu.SemaphoreType.DMA((1 + C // CH,)),
    ]
    smem = pl.BlockSpec(memory_space=pltpu.SMEM)
    vmem = pl.BlockSpec(memory_space=pltpu.VMEM)
    hbm = pl.BlockSpec(memory_space=pl.ANY)

    def body(images, texts, img_group, txt_group, temp, bias, loss_scale):
        gi, gt = pl.pallas_call(
            functools.partial(kernel, (nz, ny, nx, F, FP, C, total_images)),
            out_shape=(jax.ShapeDtypeStruct((F, C), f32), jax.ShapeDtypeStruct((R, F), f32)),
            in_specs=[hbm, vmem, smem, smem, smem, smem, smem],
            out_specs=(hbm, vmem),
            scratch_shapes=scratch,
            compiler_params=pltpu.CompilerParams(
                collective_id=0, has_side_effects=True, vmem_limit_bytes=56 * 1024 * 1024
            ),
        )(images.T, texts, img_group, txt_group, temp.reshape(1), bias.reshape(1), loss_scale.reshape(1))
        return gi.T, gt

    return body


def solution(mesh):
    body = build(NZ, NY, NX, 576, 640, 1024, 131072)
    in_specs = (P("blk", "feat"), P("blk", "feat"), P(), P(), P(), P(), P())
    out_specs = (P("blk", "feat"), P("blk", "feat"))
    return jax.shard_map(body, mesh=mesh, in_specs=in_specs, out_specs=out_specs, check_vma=False)
```

time: 988 us -> 126 us (0.13)
  waiting for transfers between devices: 938 us -> 0 us
  Pallas kernels: 0 us -> 118 us
  matrix products: 22.5 us -> 0 us
  between operations: 15.7 us -> 2.58 us
    reduce_scatter x2 -> x0, waiting for transfers between devices: 753 us -> none  [the longest x1 661 us: body(): lax.psum_scatter(jnp.dot(block, images, preferred_element_type=jnp.float3...]
    all_gather x2 -> x0, waiting for transfers between devices: 185 us -> none  [the longest x1 122 us: body(): all_texts = lax.all_gather(texts, 'blk', axis=0, tiled=True)]
    pallas_call x0 -> x1, Pallas kernels: none -> 118 us  [body(): pl.pallas_call(functools.partial(kernel, (nz, ny, nx, F, FP, C, total_ima...]
    dot_general x3 -> x0, matrix products: 22.5 us -> none  [the longest x1 7.95 us: body(): jnp.dot(block, images, preferred_element_type=jnp.float32)]
  transfers between devices with their start and end apart: 4 -> 0, of which waited for: 4 -> 0; matrix products, arithmetic and copies ran while one was open for 1% -> 0% of each run, Pallas kernels for 0% -> 0%
where the time goes in v1:
time: 126 us; the launch traced here: 125 us
  Pallas kernels  118 us (94%)
  local copies, waits for them, and re-layouts  3.99 us (3%)
  between operations  2.58 us (2%)
    pallas_call x1, Pallas kernels, body(): pl.pallas_call(functools.partial(kernel, (nz, ny, nx, F, FP, C, total_ima...  118 us
    unnamed x4, local copies, waits for them, and re-layouts  3.99 us

profile of v1, /device:TPU:8, one launch (start us, length us, event | category | flops | bytes accessed | tf_op | source)
XLA Modules:
  0.0 124.5 jit_solution(17602981913767799559)
XLA Ops:
  2.6 118.0 %shard_map.86 = (f32[576,1024]{1,0:T(8,128)}, f32[16,576]{1,0:T(8,128)}) custom-call(bf16[576,1024]{1,0:T(8,128)(2,1)} %bitcast.9, bf16[16,576]{1,0:T(8,128)(2,1)} %txt_ref.1, s32[1024]{0:T(1024)} %ig_ref.1, s32[16]{0:T(128)} %tg_ref.1, f32[1]{0:T(128)} %bitcast.5.temp_ref, f32[1]{0:T(128)} %bitcast.6.bias_ref, f32[1]{0:T(128)} %bitcast.7.scale_ref), custom_call_target="tpu_custom_call" | custom-call | tf_op jit(solution)/shard_map/pallas_call | solution.py:389
  120.5 0.0 copy-start
  120.6 3.4 %copy.14 = f32[1024,576]{0,1:T(8,128)} copy(f32[1024,576]{0,1:T(8,128)} %bitcast.8) | data formatting | bytes 4718592
  123.9 0.0 copy-done
  123.9 0.6 copy.15
Async XLA Ops:
  120.5 3.4 %copy-start = (f32[16,576]{1,0:T(8,128)S(1)}, f32[16,576]{1,0:T(8,128)}, u32[]{:S(2)}) copy-start(f32[16,576]{1,0:T(8,128)} %get-tuple-element.9) | copy-start | bytes 110596

commit v2 on v0

v2 whole, which is shorter than its diff:
```python
import functools

import jax
import jax.numpy as jnp
from jax import lax
from jax.experimental import pallas as pl
from jax.experimental.pallas import tpu as pltpu
from jax.sharding import PartitionSpec as P

MESH = pl.DeviceIdType.MESH
NZ, NY, NX = 8, 2, 4
R = 16
CH = 256
WIRE_A = jnp.float32
WIRE_B = jnp.float32


def chain_lengths(n):
    return n // 2, (n - 1) // 2


def near_first(n):
    lf, lb = chain_lengths(n)
    return sorted(range(-lf, lb + 1), key=lambda k: (abs(k), k))


def kernel(
    cfg,
    img_ref, txt_ref, ig_ref, tg_ref, temp_ref, bias_ref, scale_ref,
    gi_out, gt_out,
    T, TT, I, W, G, gI, gIr, tgv, Y,
    sAzf, sAzb, rAzf, rAzb, sBxf, sBxb, rBxf, rBxb,
    SA, rAx, SB, rBzf, rBzb, finY, rY,
    send, recv, loc,
):
    nz, ny, nx, F, C, total_images = cfg
    NCH = C // CH
    HZ = nz // 2
    TM = HZ * nx * R
    W2 = 2 * CH
    ZO, XO = near_first(nz), near_first(nx)
    lfz, lbz = chain_lengths(nz)
    lfx, lbx = chain_lengths(nx)

    def norm(k, n):
        return k - n if k > (n - 1) // 2 else k

    def zi(k):
        return ZO.index(norm(k, nz))

    def xi(k):
        return XO.index(norm(k, nx))

    blk = lax.axis_index("blk")
    feat = lax.axis_index("feat")
    core = lax.rem(blk, 2)
    x = lax.rem(blk // 2, nx)
    yh = lax.rem(blk // (2 * nx), ny)
    z = blk // (2 * nx * ny)
    step_dir = 1 - 2 * core

    def at(z_, yh_, x_, core_, feat_):
        return (((z_ * ny + yh_) * nx + x_) * 2 + core_, feat_)

    def zz(k):
        return lax.rem(z + step_dir * k + 2 * nz, nz)

    def xx(k):
        return lax.rem(x + step_dir * k + 2 * nx, nx)

    sibling = at(z, yh, x, 1 - core, feat)
    dev_f = at(z, yh, x, core, 1 - feat)
    dev_y = at(z, 1 - yh, x, core, feat)
    dev_d = at(z, 1 - yh, x, core, 1 - feat)
    zf, zb = at(zz(1), yh, x, core, feat), at(zz(-1), yh, x, core, feat)

    def xd(k):
        return at(z, yh, xx(k), core, feat)

    x_steps = [k for k in (1, -1, 2) if k < nx and (k != -1 or nx > 2)]
    barrier = pltpu.get_barrier_semaphore()
    partners = [sibling, dev_f, dev_y, dev_d, zf, zb] + [xd(k) for k in x_steps]
    for dev in partners:
        pl.semaphore_signal(barrier, inc=1, device_id=dev, device_id_type=MESH)

    ccol = pl.multiple_of(core * CH, 128)
    frow = pl.multiple_of(feat * F, 16)
    orow = pl.multiple_of((1 - feat) * F, 16)

    def img_src(j):
        return img_ref.at[:, pl.ds(j * CH, CH)]

    def img_dst(j):
        return I.at[j, pl.ds(frow, F), pl.ds(ccol, CH)]

    own_copies = [pltpu.make_async_copy(img_src(j), img_dst(j), loc.at[j]) for j in range(NCH)]
    for c in own_copies:
        c.start()
    me = yh * 2 + feat
    Y[me, :, 0:F] = txt_ref[...]
    for i, kz in enumerate(ZO):
        t, a = divmod(i, HZ)
        for h in range(2):
            group = jnp.full((nx * R, 128), tg_ref[zz(kz) * ny + h], jnp.int32)
            tgv[2 * h + t, a * nx * R : (a + 1) * nx * R, :] = group
    G[...] = jnp.zeros_like(G)

    pl.semaphore_wait(barrier, len(partners))

    count = [0]
    started = []

    def copy_to(src, dst, dev):
        i = count[0]
        count[0] += 1
        c = pltpu.make_async_remote_copy(
            src_ref=src, dst_ref=dst, send_sem=send.at[i], recv_sem=recv.at[i], device_id=dev, device_id_type=MESH
        )
        c.start()
        started.append(c)
        return c

    y_copies = [copy_to(Y.at[me], Y.at[me], dev) for dev in (dev_f, dev_y, dev_d)]
    img_copies = [copy_to(img_src(j), img_dst(j), dev_f) for j in range(NCH)]
    sib_copies = [copy_to(img_src(j), img_dst(j), sibling) for j in range(NCH)]
    fwd_copies = {}

    def forward_images(j):
        if j < NCH:
            img_copies[j].wait_recv()
            ref = I.at[j, pl.ds(orow, F), pl.ds(ccol, CH)]
            fwd_copies[j] = copy_to(ref, ref, sibling)

    ready = set()

    def images_ready(j):
        if j < NCH and j not in ready:
            ready.add(j)
            own_copies[j].wait()
            sib_copies[j].wait_recv()
            fwd_copies[j].wait_recv()

    temp, bias = temp_ref[0], bias_ref[0]
    factor = -(scale_ref[0] * temp / total_images)

    def task(m, j):
        raw = jnp.dot(T[m].reshape(TM, 2 * F), I[j], preferred_element_type=jnp.float32)
        tg = tgv[m]
        parts = []
        for q in range(W2 // 128):
            per = CH // 128
            group = ig_ref[(blk - core + q // per) * (C // 128) + j * per + q % per]
            logit = temp * raw[:, q * 128 : (q + 1) * 128] + bias
            same = tg == group
            p = 1.0 / (1.0 + jnp.exp(jnp.where(same, logit, -logit)))
            parts.append((jnp.where(same, factor, -factor) * p).astype(jnp.bfloat16))
        w = jnp.concatenate(parts, axis=1)
        W[j, m] = w
        part = lax.dot_general(
            w, I[j, pl.ds(frow, F), :], (((1,), (1,)), ((), ())), preferred_element_type=jnp.float32
        )
        G[m] = G[m] + part.reshape(HZ, nx, R, F)

    def loop_m(j, lo, hi):
        if j < NCH:
            lax.fori_loop(lo, hi, lambda m, c: (task(m, j), c)[1], 0)

    def loop_j(m, lo, hi):
        if lo < min(hi, NCH):
            lax.fori_loop(lo, min(hi, NCH), lambda j, c: (task(m, j), c)[1], 0)

    def slot(h, kz, kx):
        i = zi(kz)
        return T.at[2 * h + i // HZ, i % HZ, xi(kx)]

    for c in y_copies:
        c.wait_recv()
    for h in range(2):
        T[2 * h, 0, 0] = jnp.concatenate([Y[2 * h, :, 0:F], Y[2 * h + 1, :, 0:F]], axis=1)

    az, bz, bx, ax = {}, {}, {}, {}

    def z_send(store, h, kx, s):
        if s < lfz:
            store[kx, 1, s] = copy_to(slot(h, -s, kx), slot(h, -s - 1, kx), zf)
        if s < lbz:
            store[kx, -1, s] = copy_to(slot(h, s, kx), slot(h, s + 1, kx), zb)

    def z_wait(store, kx, s):
        for d in (1, -1):
            if (kx, d, s) in store:
                store[kx, d, s].wait_recv()

    def bx_send(kz):
        if kz in bx or kz not in ZO:
            return
        bx[kz] = [copy_to(slot(1, kz, 0), slot(1, kz, -1), xd(1))]
        if lbx:
            bx[kz].append(copy_to(slot(1, kz, 0), slot(1, kz, 1), xd(-1)))

    bx2 = {}

    def bx_fwd(kz):
        if kz in bx2 or kz not in ZO or lfx < 2:
            return
        bx[kz][0].wait_recv()
        bx2[kz] = copy_to(slot(1, kz, -1), slot(1, kz, -2), xd(1))

    def bx_fin(kz):
        if lfx < 2:
            bx[kz][0].wait_recv()
        else:
            bx2[kz].wait_recv()
        for c in bx[kz][1:]:
            c.wait_recv()

    z_send(bz, 1, 0, 0)
    for k in x_steps:
        ax[k] = copy_to(slot(0, 0, 0), slot(0, 0, -k), xd(k))
    z_send(az, 0, 0, 0)
    bx_send(0)
    others = [norm(-k, nx) for k in x_steps]
    for s in range(lfz):
        z_wait(bz, 0, s)
        z_send(bz, 1, 0, s + 1)
        bx_send(-s - 1)
        if s + 1 <= lbz:
            bx_send(s + 1)
        if s == 0:
            for k in x_steps[:2]:
                ax[k].wait_recv()
                z_send(az, 0, norm(-k, nx), 0)
            z_wait(az, 0, 0)
            z_send(az, 0, 0, 1)
            for k in x_steps[2:]:
                ax[k].wait_recv()
                z_send(az, 0, norm(-k, nx), 0)
            bx_fwd(0)
            forward_images(0)
        else:
            if s == 3:
                task(0, 0)
            for kx in others[:2]:
                z_wait(az, kx, s - 1)
                z_send(az, 0, kx, s)
            z_wait(az, 0, s)
            z_send(az, 0, 0, s + 1)
            bx_fwd(-s)
            bx_fwd(s)
            for kx in others[2:]:
                z_wait(az, kx, s - 1)
                z_send(az, 0, kx, s)
            if s == 2:
                forward_images(1)
                images_ready(0)
    if lfz < 3:
        forward_images(1)
        images_ready(0)
    if lfz < 4:
        task(0, 0)
    bx_fwd(-lfz)
    images_ready(1)
    loop_j(0, 1, 2)
    for kz in ZO[:HZ]:
        bx_fin(kz)
    loop_j(2, 0, 2)
    for kx in others:
        z_wait(az, kx, lfz - 1)
    loop_j(1, 0, 2)
    for kz in ZO[HZ:]:
        bx_fin(kz)
    forward_images(2)
    loop_j(3, 0, 2)
    images_ready(2)
    loop_m(2, 0, 4)
    forward_images(3)
    images_ready(3)

    NSUB = 2
    XS = nx // NSUB

    def azr_send(s):
        for sub in range(NSUB):
            xs = slice(sub * XS, (sub + 1) * XS)
            for d, length, sbuf, rbuf, dev in ((1, lfz, sAzf, rAzf, zf), (-1, lbz, sAzb, rAzb, zb)):
                if s >= length:
                    continue
                if s > 0:
                    azr[d, sub, s - 1].wait_recv()
                i = zi(d * (length - s))
                val = G[i // HZ, i % HZ, xs]
                if s > 0:
                    val = val + rbuf[s - 1, sub].astype(jnp.float32)
                sbuf[s, sub] = val.astype(sbuf.dtype)
                azr[d, sub, s] = copy_to(sbuf.at[s, sub], rbuf.at[s, sub], dev)

    azr = {}
    bxr = {}

    def bxr_send(s):
        for sub in range(2):
            for d, length, sbuf, rbuf in ((1, lfx, sBxf, rBxf), (-1, lbx, sBxb, rBxb)):
                if s >= length:
                    continue
                if s > 0:
                    bxr[d, sub, s - 1].wait_recv()
                val = G[2 + sub, :, xi(d * (length - s))]
                if s > 0:
                    val = val + rbuf[s - 1, sub].astype(jnp.float32)
                sbuf[s, sub] = val.astype(sbuf.dtype)
                bxr[d, sub, s] = copy_to(sbuf.at[s, sub], rbuf.at[s, sub], xd(d))

    LO = F // 128 * 128
    TW = 2 * F - LO

    def transpose_tile(m, c):
        rows = T[m].reshape(TM, 2 * F)
        own = jnp.where(feat == 0, rows[:, 0:TW], rows[:, LO : LO + TW])
        TT[m] = own.T
        return c

    def gi_step(j, c):
        off = pl.multiple_of(feat * (F - LO), 16)
        total = None
        for m in range(4):
            part = jnp.dot(TT[m, pl.ds(off, F), :], W[j, m], preferred_element_type=jnp.float32)
            total = part if total is None else total + part
        gI[j] = total
        return c

    gi_copies = []

    def gi_send(j):
        src = gI.at[j, :, pl.ds(pl.multiple_of((1 - core) * CH, 128), CH)]
        gi_copies.append(copy_to(src, gIr.at[j], sibling))

    out_copies = []

    def gi_finish(j):
        gi_copies[j].wait_recv()
        gIr[j] = gIr[j] + gI[j, :, pl.ds(ccol, CH)]
        c = pltpu.make_async_copy(gIr.at[j], gi_out.at[:, pl.ds(j * CH, CH)], loc.at[NCH + j])
        c.start()
        out_copies.append(c)

    last = NCH - 1
    early = lbz > 0 and zi(-lbz) // HZ == 1
    loop_m(last, 1, 2)
    if early:
        azr_send(0)
    loop_m(last, 2, 4)
    bxr_send(0)
    loop_m(last, 0, 1)
    if not early:
        azr_send(0)
    lax.fori_loop(0, 4, transpose_tile, 0)
    azr_send(1)
    gi_step(0, 0)
    gi_send(0)
    bxr_send(1)
    azr_send(2)
    if NCH > 1:
        gi_step(1, 0)
        gi_send(1)
    for sub in range(2):
        total = G[2 + sub, :, 0]
        for d, length, rbuf in ((1, lfx, rBxf), (-1, lbx, rBxb)):
            if length:
                bxr[d, sub, length - 1].wait_recv()
                total = total + rbuf[length - 1, sub].astype(jnp.float32)
        SB[sub] = total
    bzr = {}

    def bzr_send(s):
        for d, length, rbuf, dev in ((1, lfz, rBzf, zf), (-1, lbz, rBzb, zb)):
            if s >= length:
                continue
            i = zi(d * (length - s))
            src = SB.at[i // HZ, i % HZ]
            if s > 0:
                bzr[d, s - 1].wait_recv()
                rbuf[s - 1] = rbuf[s - 1] + src[...]
                src = rbuf.at[s - 1]
            bzr[d, s] = copy_to(src, rbuf.at[s], dev)

    bzr_send(0)
    azr_send(3)
    if NCH > 2:
        gi_step(2, 0)
        gi_send(2)
    bzr_send(1)
    for sub in range(NSUB):
        xs = slice(sub * XS, (sub + 1) * XS)
        total = G[0, 0, xs]
        for d, length, rbuf in ((1, lfz, rAzf), (-1, lbz, rAzb)):
            if length:
                azr[d, sub, length - 1].wait_recv()
                total = total + rbuf[length - 1, sub].astype(jnp.float32)
        SA[xs] = total
    axr = [copy_to(SA.at[xi(k)], rAx.at[n], xd(k)) for n, k in enumerate(x_steps)]
    if NCH > 3:
        gi_step(3, 0)
        gi_send(3)
    bzr_send(2)
    gi_finish(0)
    bzr_send(3)
    for j in range(1, NCH):
        gi_finish(j)
    endA = SA[0]
    for n, c in enumerate(axr):
        c.wait_recv()
        endA = endA + rAx[n]
    endB = SB[0, 0]
    for d, length, rbuf in ((1, lfz, rBzf), (-1, lbz, rBzb)):
        if length:
            bzr[d, length - 1].wait_recv()
            endB = endB + rbuf[length - 1]
    first = yh == 0
    finY[...] = jnp.where(first, endB, endA)
    last_copy = copy_to(finY, rY, dev_y)
    own = jnp.where(first, endA, endB)
    last_copy.wait_recv()
    gt_out[...] = own + rY[...]

    for c in started:
        c.wait_send()
    for c in out_copies:
        c.wait()


def build(nz, ny, nx, F, C, total_images):
    lfx, lbx = chain_lengths(nx)
    lfz, lbz = chain_lengths(nz)
    hz, xs = nz // 2, nx // 2
    tm = hz * nx * R
    nch = C // CH
    tw = 2 * F - F // 128 * 128
    f32, bf16 = jnp.float32, jnp.bfloat16

    def chain(n, shape, dtype):
        return pltpu.VMEM((max(n, 1),) + shape, dtype)

    scratch = [
        pltpu.VMEM((4, hz, nx, R, 2 * F), bf16),
        pltpu.VMEM((4, tw, tm), bf16),
        pltpu.VMEM((nch, 2 * F, 2 * CH), bf16),
        pltpu.VMEM((nch, 4, tm, 2 * CH), bf16),
        pltpu.VMEM((4, hz, nx, R, F), f32),
        pltpu.VMEM((nch, F, 2 * CH), f32),
        pltpu.VMEM((nch, F, CH), f32),
        pltpu.VMEM((4, tm, 128), jnp.int32),
        pltpu.VMEM((4, R, -(-F // 128) * 128), bf16),
        *[chain(n, (2, xs, R, F), WIRE_A) for n in (lfz, lbz, lfz, lbz)],
        *[chain(n, (2, hz, R, F), WIRE_B) for n in (lfx, lbx, lfx, lbx)],
        pltpu.VMEM((nx, R, F), f32),
        pltpu.VMEM((3, R, F), f32),
        pltpu.VMEM((2, hz, R, F), f32),
        chain(lfz, (R, F), f32),
        chain(lbz, (R, F), f32),
        pltpu.VMEM((R, F), f32),
        pltpu.VMEM((R, F), f32),
        pltpu.SemaphoreType.DMA((140,)),
        pltpu.SemaphoreType.DMA((140,)),
        pltpu.SemaphoreType.DMA((2 * nch,)),
    ]
    smem = pl.BlockSpec(memory_space=pltpu.SMEM)
    vmem = pl.BlockSpec(memory_space=pltpu.VMEM)
    hbm = pl.BlockSpec(memory_space=pl.ANY)

    def body(images, texts, img_group, txt_group, temp, bias, loss_scale):
        gi, gt = pl.pallas_call(
            functools.partial(kernel, (nz, ny, nx, F, C, total_images)),
            out_shape=(jax.ShapeDtypeStruct((F, C), f32), jax.ShapeDtypeStruct((R, F), f32)),
            in_specs=[hbm, vmem, smem, smem, smem, smem, smem],
            out_specs=(hbm, vmem),
            scratch_shapes=scratch,
            compiler_params=pltpu.CompilerParams(
                collective_id=0, has_side_effects=True, vmem_limit_bytes=56 * 1024 * 1024
            ),
        )(images.T, texts, img_group, txt_group, temp.reshape(1), bias.reshape(1), loss_scale.reshape(1))
        return gi.T, gt

    return body


def solution(mesh):
    body = build(NZ, NY, NX, 576, 1024, 131072)
    in_specs = (P("blk", "feat"), P("blk", "feat"), P(), P(), P(), P(), P())
    out_specs = (P("blk", "feat"), P("blk", "feat"))
    return jax.shard_map(body, mesh=mesh, in_specs=in_specs, out_specs=out_specs, check_vma=False)
```

time: 988 us -> 86.2 us (0.09)
  waiting for transfers between devices: 938 us -> 0 us
  Pallas kernels: 0 us -> 79 us
  matrix products: 22.5 us -> 0 us
  between operations: 15.7 us -> 2.58 us
    reduce_scatter x2 -> x0, waiting for transfers between devices: 753 us -> none  [the longest x1 661 us: body(): lax.psum_scatter(jnp.dot(block, images, preferred_element_type=jnp.float3...]
    all_gather x2 -> x0, waiting for transfers between devices: 185 us -> none  [the longest x1 122 us: body(): all_texts = lax.all_gather(texts, 'blk', axis=0, tiled=True)]
    pallas_call x0 -> x1, Pallas kernels: none -> 79 us  [body(): pl.pallas_call(functools.partial(kernel, (nz, ny, nx, F, C, total_images)...]
    dot_general x3 -> x0, matrix products: 22.5 us -> none  [the longest x1 7.95 us: body(): jnp.dot(block, images, preferred_element_type=jnp.float32)]
  transfers between devices with their start and end apart: 4 -> 0, of which waited for: 4 -> 0; matrix products, arithmetic and copies ran while one was open for 1% -> 0% of each run, Pallas kernels for 0% -> 0%
where the time goes in v2:
time: 86.2 us; the launch traced here: 85.6 us
  Pallas kernels  79 us (92%)
  local copies, waits for them, and re-layouts  3.99 us (5%)
  between operations  2.58 us (3%)
    pallas_call x1, Pallas kernels, body(): pl.pallas_call(functools.partial(kernel, (nz, ny, nx, F, C, total_images)...  79 us
    unnamed x4, local copies, waits for them, and re-layouts  3.99 us

profile of v2, /device:TPU:8, one launch (start us, length us, event | category | flops | bytes accessed | tf_op | source)
XLA Modules:
  0.0 85.6 jit_solution(10286113351934495336)
XLA Ops:
  2.6 79.0 %shard_map.86 = (f32[576,1024]{1,0:T(8,128)}, f32[16,576]{1,0:T(8,128)}) custom-call(bf16[576,1024]{1,0:T(8,128)(2,1)} %bitcast.9, bf16[16,576]{1,0:T(8,128)(2,1)} %txt_ref.1, s32[1024]{0:T(1024)} %ig_ref.1, s32[16]{0:T(128)} %tg_ref.1, f32[1]{0:T(128)} %bitcast.5.temp_ref, f32[1]{0:T(128)} %bitcast.6.bias_ref, f32[1]{0:T(128)} %bitcast.7.scale_ref), custom_call_target="tpu_custom_call" | custom-call | tf_op jit(solution)/shard_map/pallas_call | solution.py:471
  81.6 0.0 copy-start
  81.6 3.4 %copy.14 = f32[1024,576]{0,1:T(8,128)} copy(f32[1024,576]{0,1:T(8,128)} %bitcast.8) | data formatting | bytes 4718592
  85.0 0.0 copy-done
  85.0 0.6 copy.15
Async XLA Ops:
  81.6 3.4 %copy-start = (f32[16,576]{1,0:T(8,128)S(1)}, f32[16,576]{1,0:T(8,128)}, u32[]{:S(2)}) copy-start(f32[16,576]{1,0:T(8,128)} %get-tuple-element.9) | copy-start | bytes 110596

commit v3 on v2

--- a/solution.py
+++ b/solution.py
@@ -12,7 +12,7 @@
 R = 16
 CH = 256
 WIRE_A = jnp.float32
-WIRE_B = jnp.float32
+WIRE_B = jnp.bfloat16
 
 
 def chain_lengths(n):
@@ -26,11 +26,12 @@
 
 def kernel(
     cfg,
-    img_ref, txt_ref, ig_ref, tg_ref, temp_ref, bias_ref, scale_ref,
+    img_ref, txt_hbm, ig_hbm, tg_hbm, temp_hbm, bias_hbm, scale_hbm,
     gi_out, gt_out,
+    txt_ref, ig_ref, tg_ref, temp_ref, bias_ref, scale_ref,
     T, TT, I, W, G, gI, gIr, tgv, Y,
     sAzf, sAzb, rAzf, rAzb, sBxf, sBxb, rBxf, rBxb,
-    SA, rAx, SB, rBzf, rBzb, finY, rY,
+    SA, rAx, SB, rBz, finY, rY,
     send, recv, loc,
 ):
     nz, ny, nx, F, C, total_images = cfg
@@ -77,9 +78,22 @@
     def xd(k):
         return at(z, yh, xx(k), core, feat)
 
+    def zd(k):
+        return at(zz(k), yh, x, core, feat)
+
     x_steps = [k for k in (1, -1, 2) if k < nx and (k != -1 or nx > 2)]
+    txt_copy = pltpu.make_async_copy(txt_hbm, txt_ref, loc.at[NCH])
+    txt_copy.start()
+    small = [
+        pltpu.make_async_copy(src, dst, loc.at[NCH + 1 + n])
+        for n, (src, dst) in enumerate(
+            ((ig_hbm, ig_ref), (tg_hbm, tg_ref), (temp_hbm, temp_ref), (bias_hbm, bias_ref), (scale_hbm, scale_ref))
+        )
+    ]
+    for c in small:
+        c.start()
     barrier = pltpu.get_barrier_semaphore()
-    partners = [sibling, dev_f, dev_y, dev_d, zf, zb] + [xd(k) for k in x_steps]
+    partners = [sibling, dev_f, dev_y, dev_d, zf, zb, zd(2), zd(-2)] + [xd(k) for k in x_steps]
     for dev in partners:
         pl.semaphore_signal(barrier, inc=1, device_id=dev, device_id_type=MESH)
 
@@ -97,7 +111,10 @@
     for c in own_copies:
         c.start()
     me = yh * 2 + feat
+    txt_copy.wait()
     Y[me, :, 0:F] = txt_ref[...]
+    for c in small:
+        c.wait()
     for i, kz in enumerate(ZO):
         t, a = divmod(i, HZ)
         for h in range(2):
@@ -214,63 +231,77 @@
         for c in bx[kz][1:]:
             c.wait_recv()
 
-    z_send(bz, 1, 0, 0)
+    def bz_send(k, frm=0):
+        bz[k] = copy_to(slot(1, frm, 0), slot(1, frm - (k - SIGN[k] * abs(frm)), 0), zd(k - SIGN[k] * abs(frm)))
+
+    SIGN = {1: 1, 2: 1, 3: 1, 4: 1, -1: -1, -2: -1, -3: -1}
+    for k in (1, -1, 2, -2):
+        bz_send(k)
     for k in x_steps:
         ax[k] = copy_to(slot(0, 0, 0), slot(0, 0, -k), xd(k))
     z_send(az, 0, 0, 0)
     bx_send(0)
     others = [norm(-k, nx) for k in x_steps]
-    for s in range(lfz):
-        z_wait(bz, 0, s)
-        z_send(bz, 1, 0, s + 1)
-        bx_send(-s - 1)
-        if s + 1 <= lbz:
-            bx_send(s + 1)
-        if s == 0:
-            for k in x_steps[:2]:
-                ax[k].wait_recv()
-                z_send(az, 0, norm(-k, nx), 0)
-            z_wait(az, 0, 0)
-            z_send(az, 0, 0, 1)
-            for k in x_steps[2:]:
-                ax[k].wait_recv()
-                z_send(az, 0, norm(-k, nx), 0)
-            bx_fwd(0)
-            forward_images(0)
-        else:
-            if s == 3:
-                task(0, 0)
-            for kx in others[:2]:
-                z_wait(az, kx, s - 1)
-                z_send(az, 0, kx, s)
-            z_wait(az, 0, s)
-            z_send(az, 0, 0, s + 1)
-            bx_fwd(-s)
-            bx_fwd(s)
-            for kx in others[2:]:
-                z_wait(az, kx, s - 1)
-                z_send(az, 0, kx, s)
-            if s == 2:
-                forward_images(1)
-                images_ready(0)
-    if lfz < 3:
-        forward_images(1)
-        images_ready(0)
-    if lfz < 4:
-        task(0, 0)
-    bx_fwd(-lfz)
-    images_ready(1)
-    loop_j(0, 1, 2)
+
+    def az_on(kxs, s):
+        for kx in kxs:
+            z_wait(az, kx, s - 1)
+            z_send(az, 0, kx, s)
+
+    def bz_got(*ks):
+        for k in ks:
+            bz[k].wait_recv()
+        for k in ks:
+            bx_send(-k)
+
+    bz_got(1, -1)
+    for k in x_steps[:2]:
+        ax[k].wait_recv()
+        z_send(az, 0, norm(-k, nx), 0)
+    bz[2].wait_recv()
+    bz_send(4, -2)
+    bz_send(3, -2)
+    bz[-2].wait_recv()
+    bz_send(-3, 2)
+    az_on([0], 1)
+    bx_send(-2)
+    bx_send(2)
+    for k in x_steps[2:]:
+        ax[k].wait_recv()
+        z_send(az, 0, norm(-k, nx), 0)
+    bx_fwd(0)
+    az_on(others[:2], 1)
+    bx_fwd(-1)
+    bx_fwd(1)
+    az_on([0], 2)
+    az_on(others[2:], 1)
+    bz_got(3, -3, 4)
+    bx_fwd(-2)
+    forward_images(0)
+    az_on(others[:2], 2)
+    az_on([0], 3)
+    az_on(others[2:], 2)
     for kz in ZO[:HZ]:
         bx_fin(kz)
-    loop_j(2, 0, 2)
-    for kx in others:
-        z_wait(az, kx, lfz - 1)
-    loop_j(1, 0, 2)
+    images_ready(0)
+    task(2, 0)
+    bx_fwd(2)
+    bx_fwd(-3)
+    bx_fwd(3)
+    bx_fwd(-4)
+    az_on(others[:2], 3)
+    az_on(others[2:], 3)
+    task(0, 0)
+    forward_images(1)
     for kz in ZO[HZ:]:
         bx_fin(kz)
+    task(3, 0)
+    images_ready(1)
+    lax.fori_loop(0, 3, lambda i, c: (task(i + (i > 0), 1), c)[1], 0)
+    for kx in [0] + others:
+        z_wait(az, kx, lfz - 1)
     forward_images(2)
-    loop_j(3, 0, 2)
+    loop_j(1, 0, 2)
     images_ready(2)
     loop_m(2, 0, 4)
     forward_images(3)
@@ -334,14 +365,9 @@
         src = gI.at[j, :, pl.ds(pl.multiple_of((1 - core) * CH, 128), CH)]
         gi_copies.append(copy_to(src, gIr.at[j], sibling))
 
-    out_copies = []
-
     def gi_finish(j):
         gi_copies[j].wait_recv()
-        gIr[j] = gIr[j] + gI[j, :, pl.ds(ccol, CH)]
-        c = pltpu.make_async_copy(gIr.at[j], gi_out.at[:, pl.ds(j * CH, CH)], loc.at[NCH + j])
-        c.start()
-        out_copies.append(c)
+        gi_out[:, j * CH : (j + 1) * CH] = gIr[j] + gI[j, :, pl.ds(ccol, CH)]
 
     last = NCH - 1
     early = lbz > 0 and zi(-lbz) // HZ == 1
@@ -371,24 +397,24 @@
         SB[sub] = total
     bzr = {}
 
-    def bzr_send(s):
-        for d, length, rbuf, dev in ((1, lfz, rBzf, zf), (-1, lbz, rBzb, zb)):
-            if s >= length:
-                continue
-            i = zi(d * (length - s))
-            src = SB.at[i // HZ, i % HZ]
-            if s > 0:
-                bzr[d, s - 1].wait_recv()
-                rbuf[s - 1] = rbuf[s - 1] + src[...]
-                src = rbuf.at[s - 1]
-            bzr[d, s] = copy_to(src, rbuf.at[s], dev)
-
-    bzr_send(0)
+    def bzr_first():
+        for n, k, hop in ((0, 4, 2), (1, 3, 2), (2, -3, -2), (3, -2, -2)):
+            i = zi(k)
+            bzr[n] = copy_to(SB.at[i // HZ, i % HZ], rBz.at[n], zd(hop))
+
+    def bzr_second():
+        for n, k in ((0, 2), (1, 1), (2, -1)):
+            i = zi(k)
+            bzr[n].wait_recv()
+            rBz[n] = rBz[n] + SB[i // HZ, i % HZ]
+            bzr[4 + n] = copy_to(rBz.at[n], rBz.at[4 + n], zd(k))
+
+    bzr_first()
     azr_send(3)
     if NCH > 2:
         gi_step(2, 0)
         gi_send(2)
-    bzr_send(1)
+    bzr_second()
     for sub in range(NSUB):
         xs = slice(sub * XS, (sub + 1) * XS)
         total = G[0, 0, xs]
@@ -401,20 +427,16 @@
     if NCH > 3:
         gi_step(3, 0)
         gi_send(3)
-    bzr_send(2)
-    gi_finish(0)
-    bzr_send(3)
-    for j in range(1, NCH):
+    for j in range(NCH):
         gi_finish(j)
     endA = SA[0]
     for n, c in enumerate(axr):
         c.wait_recv()
         endA = endA + rAx[n]
     endB = SB[0, 0]
-    for d, length, rbuf in ((1, lfz, rBzf), (-1, lbz, rBzb)):
-        if length:
-            bzr[d, length - 1].wait_recv()
-            endB = endB + rbuf[length - 1]
+    for n in range(3, 7):
+        bzr[n].wait_recv()
+        endB = endB + rBz[n]
     first = yh == 0
     finY[...] = jnp.where(first, endB, endA)
     last_copy = copy_to(finY, rY, dev_y)
@@ -424,8 +446,6 @@
 
     for c in started:
         c.wait_send()
-    for c in out_copies:
-        c.wait()
 
 
 def build(nz, ny, nx, F, C, total_images):
@@ -440,7 +460,14 @@
     def chain(n, shape, dtype):
         return pltpu.VMEM((max(n, 1),) + shape, dtype)
 
+    smem = pltpu.SMEM
     scratch = [
+        pltpu.VMEM((R, F), bf16),
+        smem((C * nz * ny * nx * 2 // 128,), jnp.int32),
+        smem((nz * ny,), jnp.int32),
+        smem((1,), f32),
+        smem((1,), f32),
+        smem((1,), f32),
         pltpu.VMEM((4, hz, nx, R, 2 * F), bf16),
         pltpu.VMEM((4, tw, tm), bf16),
         pltpu.VMEM((nch, 2 * F, 2 * CH), bf16),
@@ -455,24 +482,22 @@
         pltpu.VMEM((nx, R, F), f32),
         pltpu.VMEM((3, R, F), f32),
         pltpu.VMEM((2, hz, R, F), f32),
-        chain(lfz, (R, F), f32),
-        chain(lbz, (R, F), f32),
+        pltpu.VMEM((7, R, F), f32),
         pltpu.VMEM((R, F), f32),
         pltpu.VMEM((R, F), f32),
         pltpu.SemaphoreType.DMA((140,)),
         pltpu.SemaphoreType.DMA((140,)),
-        pltpu.SemaphoreType.DMA((2 * nch,)),
+        pltpu.SemaphoreType.DMA((nch + 6,)),
     ]
-    smem = pl.BlockSpec(memory_space=pltpu.SMEM)
     vmem = pl.BlockSpec(memory_space=pltpu.VMEM)
     hbm = pl.BlockSpec(memory_space=pl.ANY)
 
     def body(images, texts, img_group, txt_group, temp, bias, loss_scale):
         gi, gt = pl.pallas_call(
             functools.partial(kernel, (nz, ny, nx, F, C, total_images)),
-            out_shape=(jax.ShapeDtypeStruct((F, C), f32), jax.ShapeDtypeStruct((R, F), f32)),
-            in_specs=[hbm, vmem, smem, smem, smem, smem, smem],
-            out_specs=(hbm, vmem),
+            out_shape=(pltpu.VMEM((F, C), f32), pltpu.VMEM((R, F), f32)),
+            in_specs=[hbm] * 7,
+            out_specs=(vmem, vmem),
             scratch_shapes=scratch,
             compiler_params=pltpu.CompilerParams(
                 collective_id=0, has_side_effects=True, vmem_limit_bytes=56 * 1024 * 1024

time: 86.2 us -> 79.9 us (0.927)
  Pallas kernels: 79 us -> 74.2 us
  local copies, waits for them, and re-layouts: 3.99 us -> 2.02 us
    pallas_call x1, Pallas kernels: 79 us -> 74.2 us  [body(): pl.pallas_call(functools.partial(kernel, (nz, ny, nx, F, C, total_images)...]
    unnamed x4 -> x2, local copies, waits for them, and re-layouts: 3.99 us -> 2.02 us
where the time goes in v3:
time: 79.9 us; the launch traced here: 78.8 us
  Pallas kernels  74.2 us (93%)
  between operations  2.58 us (3%)
  local copies, waits for them, and re-layouts  2.02 us (3%)
    pallas_call x1, Pallas kernels, body(): pl.pallas_call(functools.partial(kernel, (nz, ny, nx, F, C, total_images)...  74.2 us
    unnamed x2, local copies, waits for them, and re-layouts  2.02 us

profile of v3, /device:TPU:8, one launch (start us, length us, event | category | flops | bytes accessed | tf_op | source)
XLA Modules:
  0.0 78.8 jit_solution(14690698639141335345)
XLA Ops:
  2.6 74.2 %shard_map.86 = (f32[576,1024]{1,0:T(8,128)S(1)}, f32[16,576]{1,0:T(8,128)S(1)}) custom-call(bf16[576,1024]{1,0:T(8,128)(2,1)} %bitcast.9, bf16[16,576]{1,0:T(8,128)(2,1)} %txt_hbm.1, s32[1024]{0:T(1024)} %ig_hbm.1, s32[16]{0:T(128)} %tg_hbm.1, f32[1]{0:T(128)} %bitcast.5.temp_hbm, f32[1]{0:T(128)} %bitcast.6.bias_hbm, f32[1]{0:T(128)} %bitcast.7.scale_hbm), custom_call_target="tpu_custom_call" | custom-call | tf_op jit(solution)/shard_map/pallas_call | solution.py:496
  76.8 1.4 %copy.11 = f32[1024,576]{0,1:T(8,128)} copy(f32[1024,576]{0,1:T(8,128)S(1)} %bitcast.8) | data formatting | bytes 4718592
  78.2 0.6 copy.12

commit v4 on v3

--- a/solution.py
+++ b/solution.py
@@ -11,7 +11,7 @@
 NZ, NY, NX = 8, 2, 4
 R = 16
 CH = 256
-WIRE_A = jnp.float32
+WIRE_A = jnp.bfloat16
 WIRE_B = jnp.bfloat16
 
 
@@ -160,9 +160,9 @@
     temp, bias = temp_ref[0], bias_ref[0]
     factor = -(scale_ref[0] * temp / total_images)
 
-    def task(m, j):
-        raw = jnp.dot(T[m].reshape(TM, 2 * F), I[j], preferred_element_type=jnp.float32)
-        tg = tgv[m]
+    def task(m, j, n=1):
+        raw = jnp.dot(T[pl.ds(m, n)].reshape(n * TM, 2 * F), I[j], preferred_element_type=jnp.float32)
+        tg = tgv[pl.ds(m, n)].reshape(n * TM, 128)
         parts = []
         for q in range(W2 // 128):
             per = CH // 128
@@ -172,19 +172,11 @@
             p = 1.0 / (1.0 + jnp.exp(jnp.where(same, logit, -logit)))
             parts.append((jnp.where(same, factor, -factor) * p).astype(jnp.bfloat16))
         w = jnp.concatenate(parts, axis=1)
-        W[j, m] = w
+        W[j, pl.ds(m, n)] = w.reshape(n, TM, W2)
         part = lax.dot_general(
             w, I[j, pl.ds(frow, F), :], (((1,), (1,)), ((), ())), preferred_element_type=jnp.float32
         )
-        G[m] = G[m] + part.reshape(HZ, nx, R, F)
-
-    def loop_m(j, lo, hi):
-        if j < NCH:
-            lax.fori_loop(lo, hi, lambda m, c: (task(m, j), c)[1], 0)
-
-    def loop_j(m, lo, hi):
-        if lo < min(hi, NCH):
-            lax.fori_loop(lo, min(hi, NCH), lambda j, c: (task(m, j), c)[1], 0)
+        G[pl.ds(m, n)] = G[pl.ds(m, n)] + part.reshape(n, HZ, nx, R, F)
 
     def slot(h, kz, kx):
         i = zi(kz)
@@ -297,13 +289,14 @@
         bx_fin(kz)
     task(3, 0)
     images_ready(1)
-    lax.fori_loop(0, 3, lambda i, c: (task(i + (i > 0), 1), c)[1], 0)
+    task(2, 1, 2)
     for kx in [0] + others:
         z_wait(az, kx, lfz - 1)
     forward_images(2)
-    loop_j(1, 0, 2)
+    task(1, 0)
+    task(0, 1, 2)
     images_ready(2)
-    loop_m(2, 0, 4)
+    task(0, 2, 4)
     forward_images(3)
     images_ready(3)
 
@@ -313,17 +306,31 @@
     def azr_send(s):
         for sub in range(NSUB):
             xs = slice(sub * XS, (sub + 1) * XS)
-            for d, length, sbuf, rbuf, dev in ((1, lfz, sAzf, rAzf, zf), (-1, lbz, sAzb, rAzb, zb)):
-                if s >= length:
-                    continue
-                if s > 0:
-                    azr[d, sub, s - 1].wait_recv()
-                i = zi(d * (length - s))
-                val = G[i // HZ, i % HZ, xs]
-                if s > 0:
-                    val = val + rbuf[s - 1, sub].astype(jnp.float32)
-                sbuf[s, sub] = val.astype(sbuf.dtype)
-                azr[d, sub, s] = copy_to(sbuf.at[s, sub], rbuf.at[s, sub], dev)
+
+            def block(k):
+                i = zi(k)
+                return G[i // HZ, i % HZ, xs]
+
+            def put(key, val, sbuf, rbuf, dev):
+                sbuf[key[1], sub] = val.astype(sbuf.dtype)
+                azr[key[0], sub, key[1]] = copy_to(sbuf.at[key[1], sub], rbuf.at[key[1], sub], dev)
+
+            if s == 0:
+                put((1, 0), block(4), sAzf, rAzf, zd(2))
+                put((1, 1), block(3), sAzf, rAzf, zf)
+            elif s == 1:
+                azr[1, sub, 0].wait_recv()
+                azr[1, sub, 1].wait_recv()
+                val = block(2) + rAzf[0, sub].astype(jnp.float32) + rAzf[1, sub].astype(jnp.float32)
+                put((1, 2), val, sAzf, rAzf, zf)
+            else:
+                azr[1, sub, 2].wait_recv()
+                put((1, 3), block(1) + rAzf[2, sub].astype(jnp.float32), sAzf, rAzf, zf)
+            val = block(s - 3)
+            if s > 0:
+                azr[-1, sub, s - 1].wait_recv()
+                val = val + rAzb[s - 1, sub].astype(jnp.float32)
+            put((-1, s), val, sAzb, rAzb, zb)
 
     azr = {}
     bxr = {}
@@ -370,24 +377,29 @@
         gi_out[:, j * CH : (j + 1) * CH] = gIr[j] + gI[j, :, pl.ds(ccol, CH)]
 
     last = NCH - 1
-    early = lbz > 0 and zi(-lbz) // HZ == 1
-    loop_m(last, 1, 2)
-    if early:
-        azr_send(0)
-    loop_m(last, 2, 4)
+    bzr = {}
+
+    def bzr_first():
+        for n, k, hop in ((0, 4, 2), (1, 3, 2), (2, -3, -2), (3, -2, -2)):
+            i = zi(k)
+            bzr[n] = copy_to(SB.at[i // HZ, i % HZ], rBz.at[n], zd(hop))
+
+    def bzr_second():
+        for n, k in ((0, 2), (1, 1), (2, -1)):
+            i = zi(k)
+            bzr[n].wait_recv()
+            rBz[n] = rBz[n] + SB[i // HZ, i % HZ]
+            bzr[4 + n] = copy_to(rBz.at[n], rBz.at[4 + n], zd(k))
+
+    task(2, last, 2)
     bxr_send(0)
-    loop_m(last, 0, 1)
-    if not early:
-        azr_send(0)
+    task(0, last, 2)
+    azr_send(0)
     lax.fori_loop(0, 4, transpose_tile, 0)
-    azr_send(1)
+    bxr_send(1)
     gi_step(0, 0)
     gi_send(0)
-    bxr_send(1)
-    azr_send(2)
-    if NCH > 1:
-        gi_step(1, 0)
-        gi_send(1)
+    azr_send(1)
     for sub in range(2):
         total = G[2 + sub, :, 0]
         for d, length, rbuf in ((1, lfx, rBxf), (-1, lbx, rBxb)):
@@ -395,22 +407,11 @@
                 bxr[d, sub, length - 1].wait_recv()
                 total = total + rbuf[length - 1, sub].astype(jnp.float32)
         SB[sub] = total
-    bzr = {}
-
-    def bzr_first():
-        for n, k, hop in ((0, 4, 2), (1, 3, 2), (2, -3, -2), (3, -2, -2)):
-            i = zi(k)
-            bzr[n] = copy_to(SB.at[i // HZ, i % HZ], rBz.at[n], zd(hop))
-
-    def bzr_second():
-        for n, k in ((0, 2), (1, 1), (2, -1)):
-            i = zi(k)
-            bzr[n].wait_recv()
-            rBz[n] = rBz[n] + SB[i // HZ, i % HZ]
-            bzr[4 + n] = copy_to(rBz.at[n], rBz.at[4 + n], zd(k))
-
     bzr_first()
-    azr_send(3)
+    if NCH > 1:
+        gi_step(1, 0)
+        gi_send(1)
+    azr_send(2)
     if NCH > 2:
         gi_step(2, 0)
         gi_send(2)

time: 79.9 us -> 75.1 us (0.940)
  Pallas kernels: 74.2 us -> 70 us
    pallas_call x1, Pallas kernels: 74.2 us -> 70 us  [body(): pl.pallas_call(functools.partial(kernel, (nz, ny, nx, F, C, total_images)...]
where the time goes in v4:
time: 75.1 us; the launch traced here: 74.6 us
  Pallas kernels  70 us (93%)
  between operations  2.58 us (3%)
  local copies, waits for them, and re-layouts  2.02 us (3%)
    pallas_call x1, Pallas kernels, body(): pl.pallas_call(functools.partial(kernel, (nz, ny, nx, F, C, total_images)...  70 us
    unnamed x2, local copies, waits for them, and re-layouts  2.02 us

profile of v4, /device:TPU:8, one launch (start us, length us, event | category | flops | bytes accessed | tf_op | source)
XLA Modules:
  0.0 74.6 jit_solution(3550580877628707167)
XLA Ops:
  2.6 70.0 %shard_map.86 = (f32[576,1024]{1,0:T(8,128)S(1)}, f32[16,576]{1,0:T(8,128)S(1)}) custom-call(bf16[576,1024]{1,0:T(8,128)(2,1)} %bitcast.9, bf16[16,576]{1,0:T(8,128)(2,1)} %txt_hbm.1, s32[1024]{0:T(1024)} %ig_hbm.1, s32[16]{0:T(128)} %tg_hbm.1, f32[1]{0:T(128)} %bitcast.5.temp_hbm, f32[1]{0:T(128)} %bitcast.6.bias_hbm, f32[1]{0:T(128)} %bitcast.7.scale_hbm), custom_call_target="tpu_custom_call" | custom-call | tf_op jit(solution)/shard_map/pallas_call | solution.py:497
  72.6 1.4 %copy.11 = f32[1024,576]{0,1:T(8,128)} copy(f32[1024,576]{0,1:T(8,128)S(1)} %bitcast.8) | data formatting | bytes 4718592
  74.0 0.6 copy.12

commit v5 on v4

--- a/solution.py
+++ b/solution.py
@@ -26,12 +26,12 @@
 
 def kernel(
     cfg,
-    img_ref, txt_hbm, ig_hbm, tg_hbm, temp_hbm, bias_hbm, scale_hbm,
+    img_ref, txt_hbm, ig_hbm, tg_hbm, temp_ref, bias_ref, scale_ref,
     gi_out, gt_out,
-    txt_ref, ig_ref, tg_ref, temp_ref, bias_ref, scale_ref,
+    txt_ref, ig_ref, tg_ref,
     T, TT, I, W, G, gI, gIr, tgv, Y,
     sAzf, sAzb, rAzf, rAzb, sBxf, sBxb, rBxf, rBxb,
-    SA, rAx, SB, rBz, finY, rY,
+    SA, rAx, SB, sB1, rB1, rBz, finY, rY,
     send, recv, loc,
 ):
     nz, ny, nx, F, C, total_images = cfg
@@ -87,7 +87,7 @@
     small = [
         pltpu.make_async_copy(src, dst, loc.at[NCH + 1 + n])
         for n, (src, dst) in enumerate(
-            ((ig_hbm, ig_ref), (tg_hbm, tg_ref), (temp_hbm, temp_ref), (bias_hbm, bias_ref), (scale_hbm, scale_ref))
+            ((ig_hbm, ig_ref), (tg_hbm, tg_ref))
         )
     ]
     for c in small:
@@ -157,8 +157,8 @@
             sib_copies[j].wait_recv()
             fwd_copies[j].wait_recv()
 
-    temp, bias = temp_ref[0], bias_ref[0]
-    factor = -(scale_ref[0] * temp / total_images)
+    temp, bias = temp_ref[()], bias_ref[()]
+    factor = -(scale_ref[()] * temp / total_images)
 
     def task(m, j, n=1):
         raw = jnp.dot(T[pl.ds(m, n)].reshape(n * TM, 2 * F), I[j], preferred_element_type=jnp.float32)
@@ -296,8 +296,8 @@
     task(1, 0)
     task(0, 1, 2)
     images_ready(2)
+    forward_images(3)
     task(0, 2, 4)
-    forward_images(3)
     images_ready(3)
 
     NSUB = 2
@@ -382,13 +382,14 @@
     def bzr_first():
         for n, k, hop in ((0, 4, 2), (1, 3, 2), (2, -3, -2), (3, -2, -2)):
             i = zi(k)
-            bzr[n] = copy_to(SB.at[i // HZ, i % HZ], rBz.at[n], zd(hop))
+            sB1[n] = SB[i // HZ, i % HZ].astype(sB1.dtype)
+            bzr[n] = copy_to(sB1.at[n], rB1.at[n], zd(hop))
 
     def bzr_second():
         for n, k in ((0, 2), (1, 1), (2, -1)):
             i = zi(k)
             bzr[n].wait_recv()
-            rBz[n] = rBz[n] + SB[i // HZ, i % HZ]
+            rBz[n] = rB1[n].astype(jnp.float32) + SB[i // HZ, i % HZ]
             bzr[4 + n] = copy_to(rBz.at[n], rBz.at[4 + n], zd(k))
 
     task(2, last, 2)
@@ -435,7 +436,9 @@
         c.wait_recv()
         endA = endA + rAx[n]
     endB = SB[0, 0]
-    for n in range(3, 7):
+    bzr[3].wait_recv()
+    endB = endB + rB1[3].astype(jnp.float32)
+    for n in range(4, 7):
         bzr[n].wait_recv()
         endB = endB + rBz[n]
     first = yh == 0
@@ -466,9 +469,6 @@
         pltpu.VMEM((R, F), bf16),
         smem((C * nz * ny * nx * 2 // 128,), jnp.int32),
         smem((nz * ny,), jnp.int32),
-        smem((1,), f32),
-        smem((1,), f32),
-        smem((1,), f32),
         pltpu.VMEM((4, hz, nx, R, 2 * F), bf16),
         pltpu.VMEM((4, tw, tm), bf16),
         pltpu.VMEM((nch, 2 * F, 2 * CH), bf16),
@@ -483,12 +483,14 @@
         pltpu.VMEM((nx, R, F), f32),
         pltpu.VMEM((3, R, F), f32),
         pltpu.VMEM((2, hz, R, F), f32),
+        pltpu.VMEM((4, R, F), WIRE_B),
+        pltpu.VMEM((4, R, F), WIRE_B),
         pltpu.VMEM((7, R, F), f32),
         pltpu.VMEM((R, F), f32),
         pltpu.VMEM((R, F), f32),
         pltpu.SemaphoreType.DMA((140,)),
         pltpu.SemaphoreType.DMA((140,)),
-        pltpu.SemaphoreType.DMA((nch + 6,)),
+        pltpu.SemaphoreType.DMA((nch + 3,)),
     ]
     vmem = pl.BlockSpec(memory_space=pltpu.VMEM)
     hbm = pl.BlockSpec(memory_space=pl.ANY)
@@ -497,13 +499,13 @@
         gi, gt = pl.pallas_call(
             functools.partial(kernel, (nz, ny, nx, F, C, total_images)),
             out_shape=(pltpu.VMEM((F, C), f32), pltpu.VMEM((R, F), f32)),
-            in_specs=[hbm] * 7,
+            in_specs=[hbm] * 4 + [pl.BlockSpec(memory_space=pltpu.SMEM)] * 3,
             out_specs=(vmem, vmem),
             scratch_shapes=scratch,
             compiler_params=pltpu.CompilerParams(
                 collective_id=0, has_side_effects=True, vmem_limit_bytes=56 * 1024 * 1024
             ),
-        )(images.T, texts, img_group, txt_group, temp.reshape(1), bias.reshape(1), loss_scale.reshape(1))
+        )(images.T, texts, img_group, txt_group, temp, bias, loss_scale)
         return gi.T, gt
 
     return body

time: 75.1 us -> 71.2 us (0.948)
  Pallas kernels: 70 us -> 66.2 us
    pallas_call x1, Pallas kernels: 70 us -> 66.2 us  [body(): pl.pallas_call(functools.partial(kernel, (nz, ny, nx, F, C, total_images)...]
where the time goes in v5:
time: 71.2 us; the launch traced here: 70.8 us
  Pallas kernels  66.2 us (93%)
  between operations  2.58 us (4%)
  local copies, waits for them, and re-layouts  2.02 us (3%)
    pallas_call x1, Pallas kernels, body(): pl.pallas_call(functools.partial(kernel, (nz, ny, nx, F, C, total_images)...  66.2 us
    unnamed x2, local copies, waits for them, and re-layouts  2.02 us

profile of v5, /device:TPU:8, one launch (start us, length us, event | category | flops | bytes accessed | tf_op | source)
XLA Modules:
  0.0 70.8 jit_solution(4632075253944437398)
XLA Ops:
  2.6 66.2 %shard_map.86 = (f32[576,1024]{1,0:T(8,128)S(1)}, f32[16,576]{1,0:T(8,128)S(1)}) custom-call(bf16[576,1024]{1,0:T(8,128)(2,1)} %bitcast.3, bf16[16,576]{1,0:T(8,128)(2,1)} %txt_hbm.1, s32[1024]{0:T(1024)} %ig_hbm.1, s32[16]{0:T(128)} %tg_hbm.1, f32[]{:T(128)S(6)} %copy.13.temp_ref, f32[]{:T(128)S(6)} %copy.14.bias_ref, f32[]{:T(128)S(6)} %copy.15.scale_ref), custom_call_target="tpu_custom_call" | custom-call | tf_op jit(solution)/shard_map/pallas_call | solution.py:499
  68.8 1.4 %copy.11 = f32[1024,576]{0,1:T(8,128)} copy(f32[1024,576]{0,1:T(8,128)S(1)} %bitcast.2) | data formatting | bytes 4718592
  70.2 0.6 copy.12

commit v6 on v5

--- a/solution.py
+++ b/solution.py
@@ -273,21 +273,20 @@
     az_on(others[:2], 2)
     az_on([0], 3)
     az_on(others[2:], 2)
-    for kz in ZO[:HZ]:
-        bx_fin(kz)
-    images_ready(0)
-    task(2, 0)
     bx_fwd(2)
     bx_fwd(-3)
     bx_fwd(3)
     bx_fwd(-4)
+    images_ready(0)
+    task(0, 0)
     az_on(others[:2], 3)
     az_on(others[2:], 3)
-    task(0, 0)
     forward_images(1)
+    for kz in ZO[:HZ]:
+        bx_fin(kz)
     for kz in ZO[HZ:]:
         bx_fin(kz)
-    task(3, 0)
+    task(2, 0, 2)
     images_ready(1)
     task(2, 1, 2)
     for kx in [0] + others:

time: 71.2 us -> 70.2 us (0.986)
  Pallas kernels: 66.2 us -> 65.4 us
    pallas_call x1, Pallas kernels: 66.2 us -> 65.4 us  [body(): pl.pallas_call(functools.partial(kernel, (nz, ny, nx, F, C, total_images)...]
where the time goes in v6:
time: 70.2 us; the launch traced here: 70 us
  Pallas kernels  65.4 us (93%)
  between operations  2.58 us (4%)
  local copies, waits for them, and re-layouts  2.02 us (3%)
    pallas_call x1, Pallas kernels, body(): pl.pallas_call(functools.partial(kernel, (nz, ny, nx, F, C, total_images)...  65.4 us
    unnamed x2, local copies, waits for them, and re-layouts  2.02 us

profile of v6, /device:TPU:8, one launch (start us, length us, event | category | flops | bytes accessed | tf_op | source)
XLA Modules:
  0.0 70.0 jit_solution(9723017606735574139)
XLA Ops:
  2.6 65.4 %shard_map.86 = (f32[576,1024]{1,0:T(8,128)S(1)}, f32[16,576]{1,0:T(8,128)S(1)}) custom-call(bf16[576,1024]{1,0:T(8,128)(2,1)} %bitcast.3, bf16[16,576]{1,0:T(8,128)(2,1)} %txt_hbm.1, s32[1024]{0:T(1024)} %ig_hbm.1, s32[16]{0:T(128)} %tg_hbm.1, f32[]{:T(128)S(6)} %copy.13.temp_ref, f32[]{:T(128)S(6)} %copy.14.bias_ref, f32[]{:T(128)S(6)} %copy.15.scale_ref), custom_call_target="tpu_custom_call" | custom-call | tf_op jit(solution)/shard_map/pallas_call | solution.py:498
  68.0 1.4 %copy.11 = f32[1024,576]{0,1:T(8,128)} copy(f32[1024,576]{0,1:T(8,128)S(1)} %bitcast.2) | data formatting | bytes 4718592
  69.4 0.6 copy.12

commit v7 on v6

--- a/solution.py
+++ b/solution.py
@@ -288,15 +288,16 @@
         bx_fin(kz)
     task(2, 0, 2)
     images_ready(1)
+    forward_images(2)
     task(2, 1, 2)
+    images_ready(2)
+    task(2, 2, 2)
     for kx in [0] + others:
         z_wait(az, kx, lfz - 1)
-    forward_images(2)
     task(1, 0)
     task(0, 1, 2)
-    images_ready(2)
     forward_images(3)
-    task(0, 2, 4)
+    task(0, 2, 2)
     images_ready(3)
 
     NSUB = 2

time: 70.2 us -> 71.5 us (1.019)
  Pallas kernels: 65.4 us -> 66.8 us
    pallas_call x1, Pallas kernels: 65.4 us -> 66.8 us  [body(): pl.pallas_call(functools.partial(kernel, (nz, ny, nx, F, C, total_images)...]
where the time goes in v7:
time: 71.5 us; the launch traced here: 71.4 us
  Pallas kernels  66.8 us (93%)
  between operations  2.58 us (4%)
  local copies, waits for them, and re-layouts  2.02 us (3%)
    pallas_call x1, Pallas kernels, body(): pl.pallas_call(functools.partial(kernel, (nz, ny, nx, F, C, total_images)...  66.8 us
    unnamed x2, local copies, waits for them, and re-layouts  2.02 us

profile of v7, /device:TPU:8, one launch (start us, length us, event | category | flops | bytes accessed | tf_op | source)
XLA Modules:
  0.0 71.4 jit_solution(11960866462855236446)
XLA Ops:
  2.6 66.8 %shard_map.86 = (f32[576,1024]{1,0:T(8,128)S(1)}, f32[16,576]{1,0:T(8,128)S(1)}) custom-call(bf16[576,1024]{1,0:T(8,128)(2,1)} %bitcast.3, bf16[16,576]{1,0:T(8,128)(2,1)} %txt_hbm.1, s32[1024]{0:T(1024)} %ig_hbm.1, s32[16]{0:T(128)} %tg_hbm.1, f32[]{:T(128)S(6)} %copy.13.temp_ref, f32[]{:T(128)S(6)} %copy.14.bias_ref, f32[]{:T(128)S(6)} %copy.15.scale_ref), custom_call_target="tpu_custom_call" | custom-call | tf_op jit(solution)/shard_map/pallas_call | solution.py:499
  69.3 1.4 %copy.11 = f32[1024,576]{0,1:T(8,128)} copy(f32[1024,576]{0,1:T(8,128)S(1)} %bitcast.2) | data formatting | bytes 4718592
  70.7 0.6 copy.12
